TPU v7x, 512 devices: a whole 4x4x16 slice. The times are simulated.
512 devices in a mesh: role: 4 (over y_lo, core), shard: 128 (over y_hi, z, x).
Axes of the slice: x: 4, y: 4 (y_hi: 2, y_lo: 2; y = y_hi * 2 + y_lo), z: 16, core: 2. Of those that a mesh axis runs over, the one named last changes fastest.
Arguments:
- history: bfloat16 [128, 128, 1536], P('shard'), may hold values from -10 to 10
- lengths: int32 [128], P('shard'), may hold values from 1 to 128, 10240 in all
- beam_ids: int32 [128, 4, 32], P('shard', 'role'), may hold values from 0 to 255
- routes: int32 [128, 4, 32, 2], P('shard', 'role'), may hold values from 0 to 63, all different within a row; in each aligned block of 32 rows (0 to 31, 32 to 63, ..., all dimensions but the last counted through in order) at most 2 rows name the same one
- code_table: bfloat16 [1024, 1536], P('role'), may hold values from -8 to 8
- w_key: bfloat16 [1536, 1536], P('shard', 'role'), may hold values from -1 to 1
- w_value: bfloat16 [1536, 1536], P('shard', 'role'), may hold values from -0.15625 to 0.15625
- w_query: bfloat16 [1536, 1536], P('shard', 'role'), may hold values from -9 to 9
- w_out: bfloat16 [1536, 1536], P('role', 'shard'), may hold values from -0.15625 to 0.15625
- norm_gain: float32 [1536], replicated, may hold values from 0.5 to 1.5
- moe_gain: float32 [1536], replicated, may hold values from 0.5 to 1.5
- w_router: bfloat16 [1536, 64], replicated, may hold values from -0.15625 to 0.15625
- w_gate: bfloat16 [512, 1536, 384], P(('role', 'shard')), may hold values from -0.15625 to 0.15625
- w_up: bfloat16 [512, 1536, 384], P(('role', 'shard')), may hold values from -0.15625 to 0.15625
- w_down: bfloat16 [512, 384, 1536], P(('role', 'shard')), may hold values from -0.109375 to 0.109375
Outputs:
- layer_out: bfloat16 [128, 4, 32, 1536], P('shard', 'role')
Inputs may be any that keep to these rules, and one draw needn't show every extreme that they name: `lengths`: at most 128, and some request has exactly 128. `routes`: each row names two different experts; among the 32 rows of one request and level no expert is named more than 2 times, a bound that some block reaches.
All inputs are finite; a program needn't handle non-finite values. No bound on the sum of `lengths` on one device may be relied on, other than what follows from the above.
Results may differ from a plain program's by a relative error of at most 0.015.
Values may be sent and summed in bfloat16 or wider, within the bound.
A program may use at most 64 MiB of HBM per device.

v0:
```python
import jax
import jax.numpy as jnp
from jax import lax
from jax.sharding import PartitionSpec as P

D = 1536
HEADS = 24


eps = 1e-06


def norm_rows(values, scale_vec):
    values = values.astype(jnp.float32)
    power = jnp.mean(values * values, axis=-1, keepdims=True)
    return values * lax.rsqrt(power + eps) * scale_vec


def shards(
    history,
    lengths,
    beam_ids,
    routes,
    code_table,
    w_key,
    w_value,
    w_query,
    w_out,
    norm_gain,
    moe_gain,
    w_router,
    w_gate,
    w_up,
    w_down,
):
    role_count = lax.axis_size("role")
    shard_count = lax.axis_size("shard")
    expert_count = w_router.shape[1]
    slice_count = role_count * shard_count // expert_count
    beam_count = beam_ids.shape[2]
    width = code_table.shape[1]
    capacity = max(2, 4 * beam_count // expert_count)
    head_dim = D // HEADS
    key_full, value_full, query_full, out_full = (
        lax.all_gather(w_key, "shard", axis=0, tiled=True),
        lax.all_gather(w_value, "shard", axis=0, tiled=True),
        lax.all_gather(w_query, "shard", axis=0, tiled=True),
        lax.all_gather(w_out, "shard", axis=1, tiled=True),
    )
    codes_here = beam_ids[0, 0]
    lookup = (
        codes_here[:, None] == jnp.arange(code_table.shape[0], dtype=jnp.int32)[None, :]
    ).astype(jnp.bfloat16)
    own_embed = jnp.dot(lookup, code_table, preferred_element_type=jnp.float32).astype(jnp.bfloat16)
    all_embed = lax.all_gather(own_embed, "role", axis=0, tiled=True)
    normed = norm_rows(all_embed, norm_gain).astype(jnp.bfloat16)
    events = history[0]
    keys = jnp.dot(events, key_full, preferred_element_type=jnp.float32).astype(jnp.bfloat16)
    values = jnp.dot(events, value_full, preferred_element_type=jnp.float32).astype(jnp.bfloat16)
    queries = jnp.dot(normed, query_full, preferred_element_type=jnp.float32).astype(jnp.bfloat16)
    local_heads = queries.shape[1] // head_dim
    query_heads = queries.reshape(-1, local_heads, head_dim)
    key_heads = keys.reshape(-1, local_heads, head_dim)
    value_heads = values.reshape(-1, local_heads, head_dim)
    scores = jnp.einsum(
        "rhd,jhd->hrj", query_heads, key_heads, preferred_element_type=jnp.float32
    ) * head_dim ** (-0.5)
    visible = jnp.arange(events.shape[0], dtype=jnp.int32) < lengths[0]
    scores = jnp.where(visible[None, None, :], scores, -1e30)
    top_score = jnp.max(scores, axis=-1, keepdims=True)
    weights = jnp.exp(scores - top_score)
    probs = (weights / jnp.sum(weights, axis=-1, keepdims=True)).astype(jnp.bfloat16)
    mixed = jnp.einsum(
        "hrj,jhd->rhd", probs, value_heads, preferred_element_type=jnp.float32
    ).astype(jnp.bfloat16)
    partial_out = jnp.dot(
        mixed.reshape(-1, local_heads * head_dim), out_full, preferred_element_type=jnp.float32
    )
    own_sum = lax.psum_scatter(
        partial_out.astype(jnp.bfloat16), "role", scatter_dimension=0, tiled=True
    ).astype(jnp.float32)
    hidden = (own_embed.astype(jnp.float32) + own_sum).astype(jnp.bfloat16)
    moe_in = norm_rows(hidden, moe_gain).astype(jnp.bfloat16)
    logits = jnp.dot(moe_in, w_router, preferred_element_type=jnp.float32)
    route_here = routes[0, 0]
    expert_iota = jnp.arange(expert_count, dtype=jnp.int32)
    chooser = route_here[:, :, None] == expert_iota[None, None, :]
    picked = jnp.sum(jnp.where(chooser, logits[:, None, :], 0.0), axis=-1)
    gates = jax.nn.softmax(picked, axis=-1)
    flat_routes = route_here.reshape(-1)
    member = (flat_routes[:, None] == expert_iota[None, :]).astype(jnp.int32)
    before = jnp.cumsum(member, axis=0) - member
    slot_index = jnp.sum(before * member, axis=-1)
    position = flat_routes * capacity + slot_index
    placing = position[:, None] == jnp.arange(expert_count * capacity, dtype=jnp.int32)[None, :]
    doubled = jnp.repeat(moe_in, 2, axis=0)
    packed = jnp.dot(
        placing.T.astype(jnp.bfloat16), doubled, preferred_element_type=jnp.float32
    ).astype(jnp.bfloat16)
    packed = packed.reshape(expert_count, capacity, width)
    outgoing = jnp.broadcast_to(packed[:, None], (expert_count, slice_count, capacity, width))
    outgoing = outgoing.reshape(role_count, shard_count, capacity, width)
    arrived = lax.all_to_all(
        lax.all_to_all(outgoing, "role", split_axis=0, concat_axis=0, tiled=True),
        "shard",
        split_axis=1,
        concat_axis=1,
        tiled=True,
    )
    flat_rows = arrived.reshape(-1, width)
    gate_val = jnp.dot(flat_rows, w_gate[0], preferred_element_type=jnp.float32)
    up_val = jnp.dot(flat_rows, w_up[0], preferred_element_type=jnp.float32)
    inner = (jax.nn.silu(gate_val) * up_val).astype(jnp.bfloat16)
    result_rows = jnp.dot(inner, w_down[0], preferred_element_type=jnp.float32).astype(jnp.bfloat16)
    returned = lax.all_to_all(
        lax.all_to_all(
            result_rows.reshape(arrived.shape), "role", split_axis=0, concat_axis=0, tiled=True
        ),
        "shard",
        split_axis=1,
        concat_axis=1,
        tiled=True,
    )
    expert_out = (
        returned.reshape(expert_count, slice_count, capacity, width)
        .astype(jnp.float32)
        .sum(axis=1)
        .astype(jnp.bfloat16)
    )
    placing_pairs = placing.reshape(beam_count, 2, expert_count * capacity)
    weighting = jnp.sum(jnp.where(placing_pairs, gates[:, :, None], 0.0), axis=1)
    mixed_out = jnp.dot(
        weighting,
        expert_out.reshape(-1, width).astype(jnp.float32),
        precision=lax.Precision.HIGHEST,
        preferred_element_type=jnp.float32,
    )
    result = (hidden.astype(jnp.float32) + mixed_out).astype(jnp.bfloat16)
    return result.reshape(1, 1, beam_count, width)


def solution(mesh):
    return jax.shard_map(
        shards,
        mesh=mesh,
        in_specs=(
            P("shard", None, None),
            P("shard"),
            P("shard", "role", None),
            P("shard", "role", None, None),
            P("role", None),
            P("shard", "role"),
            P("shard", "role"),
            P("shard", "role"),
            P("role", "shard"),
            P(),
            P(),
            P(),
            P(("role", "shard"), None, None),
            P(("role", "shard"), None, None),
            P(("role", "shard"), None, None),
        ),
        out_specs=P("shard", "role", None, None),
        check_vma=False,
    )
```

profile of v0, /device:TPU:1, one launch (start us, length us, event | category | flops | bytes accessed | tf_op | source)
XLA Modules:
  0.0 1282.6 jit_solution(8856137596606419470)
XLA Ops:
  6.5 0.7 all-gather.13.cloned.1.call-update
  7.3 0.7 all-gather.9.cloned.1.call-update
  8.1 0.7 all-gather.11.cloned.1.call-update
  10.0 1.4 convolution_convert_fusion.3
  11.4 12.9 %all_gather.16 = bf16[128,1536]{1,0:T(8,128)(2,1)S(1)} all-gather(bf16[32,1536]{1,0:T(8,128)(2,1)S(1)} %convolution_convert_fusion.3), channel_id=1, replica_groups=mesh['role'=4,'shard'=128] {'role'}, dimensions={0}, use_global_device_ids=true | all-gather | bytes 491520 | tf_op jit(solution)/shard_map/all_gather | solution.py:55
  24.5 180.5 %all-gather.13.cloned.1.call-done = bf16[128,12,384]{2,1,0:T(8,128)(2,1)} async-done(((bf16[1,12,384]{2,1,0:T(8,128)(2,1)}), bf16[128,12,384]{2,1,0:T(8,128)(2,1)}) %all-gather.13.cloned.1.call-update) | async-done | bytes 1179664 | tf_op jit(solution)/shard_map/all_gather | solution.py:45
  205.0 2.3 reshape.132
  207.8 193.2 %all-gather.9.cloned.1.call-done = bf16[128,12,384]{2,1,0:T(8,128)(2,1)} async-done(((bf16[1,12,384]{2,1,0:T(8,128)(2,1)}), bf16[128,12,384]{2,1,0:T(8,128)(2,1)}) %all-gather.9.cloned.1.call-update) | async-done | bytes 1179664 | tf_op jit(solution)/shard_map/all_gather | solution.py:46
  400.9 2.3 reshape.128
  403.7 193.2 %all-gather.11.cloned.1.call-done = bf16[128,12,384]{2,1,0:T(8,128)(2,1)} async-done(((bf16[1,12,384]{2,1,0:T(8,128)(2,1)}), bf16[128,12,384]{2,1,0:T(8,128)(2,1)}) %all-gather.11.cloned.1.call-update) | async-done | bytes 1179664 | tf_op jit(solution)/shard_map/all_gather | solution.py:47
  596.9 2.3 reshape.130
  600.6 192.1 %all-gather.15.cloned.1.call-done = bf16[128,12,384]{2,1,0:T(8,128)(2,1)} async-done(((bf16[1,12,384]{2,1,0:T(8,128)(2,1)}), bf16[128,12,384]{2,1,0:T(8,128)(2,1)}) %all-gather.15.cloned.1.call-update) | async-done | bytes 1179664 | tf_op jit(solution)/shard_map/all_gather | solution.py:48
  792.7 2.3 reshape.134
  795.0 1.2 convolution_convert_fusion.2
  796.8 29.0 %reduce-scatter.2.cloned.1.call-done = bf16[32,1536]{1,0:T(8,128)(2,1)} async-done(((bf16[128,1536]{1,0:T(8,128)(2,1)}), bf16[32,1536]{1,0:T(8,128)(2,1)}) %reduce-scatter.2.cloned.1.call-update) | async-done | bytes 98320 | tf_op jit(solution)/shard_map/reduce_scatter | solution.py:79
  825.9 1.0 fusion.21
  826.9 1.0 fusion.23
  829.3 38.5 %all_to_all.20 = bf16[4,128,2,1536]{3,1,2,0:T(8,128)(2,1)S(1)} all-to-all(bf16[4,128,2,1536]{3,1,2,0:T(8,128)(2,1)S(1)} %copy.90), channel_id=1, replica_groups=mesh['role'=4,'shard'=128] {'role'}, dimensions={0} | all-to-all | bytes 6291456 | tf_op jit(solution)/shard_map/all_to_all | solution.py:104
  867.8 3.2 copy.91
  871.1 162.9 %all_to_all.21 = bf16[4,128,2,1536]{3,2,0,1:T(2,128)(2,1)S(1)} all-to-all(bf16[4,128,2,1536]{3,2,0,1:T(2,128)(2,1)S(1)} %copy.91), channel_id=1, replica_groups=mesh['role'=4,'shard'=128] {'shard'}, dimensions={1} | all-to-all | bytes 6291456 | tf_op jit(solution)/shard_map/all_to_all | solution.py:103
  1034.0 3.9 copy.92
  1037.9 7.5 reshape.122
  1045.4 5.1 fusion.8
  1050.5 7.8 convolution_convert_fusion
  1058.3 7.2 reshape.123
  1065.6 44.2 %all_to_all.22 = bf16[4,128,2,1536]{3,2,1,0:T(2,128)(2,1)S(1)} all-to-all(bf16[4,128,2,1536]{3,2,1,0:T(2,128)(2,1)} %reshape.123), channel_id=1, replica_groups=mesh['role'=4,'shard'=128] {'role'}, dimensions={0} | all-to-all | bytes 6291456 | tf_op jit(solution)/shard_map/all_to_all | solution.py:116
  1109.7 3.9 copy.93
  1113.6 7.6 all-to-all-start.3
  1122.0 143.8 %all-to-all-done.3 = bf16[4,128,2,1536]{3,2,0,1:T(2,128)(2,1)} async-done(((bf16[4,128,2,1536]{3,2,0,1:T(2,128)(2,1)}), bf16[4,128,2,1536]{3,2,0,1:T(2,128)(2,1)}, u32[]{:S(2)}, u32[]{:S(2)}) %all-to-all-start.3) | async-done | bytes 3145760 | tf_op jit(solution)/shard_map/all_to_all | solution.py:115
  1265.7 4.5 copy.94
  1270.2 4.0 reduce_sum.85
  1275.2 0.9 fusion.2
  (58 shorter events, 6.7 us)
Async XLA Ops:
  6.5 1044.0 %copy-start = (bf16[1,384,1536]{2,1,0:T(8,128)(2,1)S(1)}, bf16[1,384,1536]{2,1,0:T(8,128)(2,1)}, u32[]{:S(2)}) copy-start(bf16[1,384,1536]{2,1,0:T(8,128)(2,1)} %param.29) | copy-start | bytes 3538948
  6.5 198.4 %all-gather.13.cloned.1.call-start = ((), (), s32[]{:S(2)}) async-start(), calls=%async_computation.8 | async-start | bytes 1585152 | tf_op jit(solution)/shard_map/all_gather | solution.py:45
  7.3 393.7 %all-gather.9.cloned.1.call-start = ((), (), s32[]{:S(2)}) async-start(), calls=%async_computation.6 | async-start | bytes 1585152 | tf_op jit(solution)/shard_map/all_gather | solution.py:46
  8.0 588.9 %all-gather.11.cloned.1.call-start = ((), (), s32[]{:S(2)}) async-start(), calls=%async_computation.7 | async-start | bytes 1585152 | tf_op jit(solution)/shard_map/all_gather | solution.py:47
  8.7 784.0 %all-gather.15.cloned.1.call-start = ((), (), s32[]{:S(2)}) async-start(), calls=%async_computation.9 | async-start | bytes 1585152 | tf_op jit(solution)/shard_map/all_gather | solution.py:48
  9.3 816.6 %reduce-scatter.2.cloned.1.call-start = ((), (), s32[]{:S(2)}) async-start(), calls=%async_computation.5 | async-start | bytes 491520 | tf_op jit(solution)/shard_map/reduce_scatter | solution.py:79
  24.3 182.9 %copy-start.1 = (bf16[1,128,1536]{2,1,0:T(8,128)(2,1)S(1)}, bf16[1,128,1536]{2,1,0:T(8,128)(2,1)}, u32[]{:S(2)}) copy-start(bf16[1,128,1536]{2,1,0:T(8,128)(2,1)} %param.15) | copy-start | bytes 1179652
  403.6 195.6 %copy-start.6 = (f32[1536]{0:T(1024)S(1)}, f32[1536]{0:T(1024)}, u32[]{:S(2)}) copy-start(f32[1536]{0:T(1024)} %param.24) | copy-start | bytes 18436
  795.0 1.3 copy-start.4
  795.0 32.0 %copy-start.5 = (f32[1536]{0:T(1024)S(1)}, f32[1536]{0:T(1024)}, u32[]{:S(2)}) copy-start(f32[1536]{0:T(1024)} %param.25) | copy-start | bytes 18436
  1113.6 7.8 copy-start.3
  1113.6 152.1 %all-to-all-start.3 = ((bf16[4,128,2,1536]{3,2,0,1:T(2,128)(2,1)}), bf16[4,128,2,1536]{3,2,0,1:T(2,128)(2,1)}, u32[]{:S(2)}, u32[]{:S(2)}) async-start(bf16[4,128,2,1536]{3,2,0,1:T(2,128)(2,1)} %copy.93), calls=%async_computation.4 | async-start | bytes 6291456 | tf_op jit(solution)/shard_map/all_to_all | solution.py:115
  1274.3 0.9 copy-start.2
Sparse Core Ops, SparseCore 0:
  11.7 193.2 all-gather.12
  209.3 191.5 all-gather.8
  405.2 191.6 all-gather.10
  601.0 191.6 all-gather.14
  796.4 29.4 reduce-scatter.1
where the time goes:
time: 1290 us; the launch traced here: 1280 us
  waiting for transfers between devices  934 us (72%)
  blocking collectives  258 us (20%)
  local copies, waits for them, and re-layouts  41.8 us (3%)
  matrix products  19.1 us (1%)
  between operations  14.1 us (1%)
    all_gather x1, waiting for transfers between devices, shards(): lax.all_gather(w_query, 'shard', axis=0, tiled=True)  193 us
    all_gather x1, waiting for transfers between devices, shards(): lax.all_gather(w_value, 'shard', axis=0, tiled=True)  193 us
    all_gather x1, waiting for transfers between devices, shards(): lax.all_gather(w_out, 'shard', axis=1, tiled=True)  192 us
    all_gather x1, waiting for transfers between devices, shards(): lax.all_gather(w_key, 'shard', axis=0, tiled=True)  181 us
    all_to_all x1, blocking collectives, shards(): lax.all_to_all(lax.all_to_all(outgoing, 'role', split_axis=0, concat_axis...  163 us
    all_to_all x1, waiting for transfers between devices, shards(): lax.all_to_all(lax.all_to_all(result_rows.reshape(arrived.shape), 'role',...  144 us
    all_to_all x1, blocking collectives, shards(): lax.all_to_all(result_rows.reshape(arrived.shape), 'role', split_axis=0,...  44.2 us
    all_to_all x1, blocking collectives, shards(): lax.all_to_all(outgoing, 'role', split_axis=0, concat_axis=0, tiled=True)  38.5 us
  transfers between devices with their start and end apart: 6, of which 6 were waited for; matrix products, arithmetic and copies ran while one was open for 1% of the time, Pallas kernels for 0%

commit v1 on v0

v1 whole, which is shorter than its diff:
```python
import functools

import jax
import jax.numpy as jnp
from jax import lax
from jax.experimental import pallas as pl
from jax.experimental.pallas import tpu as pltpu
from jax.sharding import PartitionSpec as P

MESH = pl.DeviceIdType.MESH
F32, BF16, I32 = jnp.float32, jnp.bfloat16, jnp.int32
D = 1536
HEAD = 64
OWN = 384
ROWS = 32
EPS = 1e-06


class Here:
    def __init__(self):
        role, shard = lax.axis_index("role"), lax.axis_index("shard")
        self.role = role
        self.y_lo, self.core = role // 2, role % 2
        self.y_hi, self.z, self.x = shard // 64, (shard // 4) % 16, shard % 4
        self.y = self.y_hi * 2 + self.y_lo

    def to(self, y_hi=None, y_lo=None, core=None, z=None, x=None):
        pick = lambda new, old: old if new is None else new
        y_hi, y_lo, core = pick(y_hi, self.y_hi), pick(y_lo, self.y_lo), pick(core, self.core)
        z, x = pick(z, self.z), pick(x, self.x)
        return (y_lo * 2 + core, y_hi * 64 + z * 4 + x)


def put(src, dst, send, recv, to):
    pltpu.make_async_remote_copy(
        src_ref=src, dst_ref=dst, send_sem=send, recv_sem=recv, device_id=to, device_id_type=MESH
    ).start()


def put_or_keep(is_self, src, dst, send, recv, to):
    @pl.when(is_self)
    def _():
        pltpu.make_async_copy(src, dst, recv).start()

    @pl.when(jnp.logical_not(is_self))
    def _():
        put(src, dst, send, recv, to)


def done(ref, sem):
    pltpu.make_async_copy(ref, ref, sem).wait()


def done_unless(is_self, ref, sem):
    @pl.when(jnp.logical_not(is_self))
    def _():
        done(ref, sem)


def greet(targets):
    barrier = pltpu.get_barrier_semaphore()
    for to in targets:
        pl.semaphore_signal(barrier, inc=1, device_id=to, device_id_type=MESH)
    pl.semaphore_wait(barrier, len(targets))


def norm_rows(values, gain):
    power = jnp.mean(values * values, axis=-1, keepdims=True)
    return (values * lax.rsqrt(power + EPS) * gain).astype(BF16)


def mm(a, b):
    return jnp.dot(a, b, preferred_element_type=F32)


def mm_nt(a, b):
    return lax.dot_general(a, b, (((1,), (1,)), ((), ())), preferred_element_type=F32)


def iota(shape, dim):
    return lax.broadcasted_iota(I32, shape, dim)


def attend_kernel(
    ids, lens, gain, piece, table, hist,
    hidden,
    emb, every, events, len_out, len_in, by_x, w, part, parts,
    x_send, x_recv, e_send, e_recv, h_send, h_recv, f_send, f_recv, b_send, b_recv,
    c_send, c_recv, r_send, r_recv,
):
    me = Here()
    straight = me.y_hi == me.core
    column = []
    for k in range(8):
        if k:
            d = (me.y * 2 + me.core + k) % 8
            column.append(me.to(y_hi=d // 4, y_lo=(d // 2) % 2, core=d % 2))
    rows_x = [me.to(y_hi=me.core, core=me.y_hi, x=(me.x + k) % 4) for k in range(4)]
    up, down = me.to(z=(me.z + 1) % 16), me.to(z=(me.z + 15) % 16)
    other = me.to(core=1 - me.core)
    greet(column + rows_x[1:] + [up, down])

    for k in range(4):
        args = (piece, by_x.at[me.x], x_send.at[k], x_recv.at[me.x], rows_x[k])
        if k:
            put(*args)
        else:
            put_or_keep(straight, *args)

    len_out[...] = jnp.full((8, 128), lens[0], I32)
    put_or_keep(straight, hist, events, h_send.at[0], h_recv.at[0], rows_x[0])
    put_or_keep(straight, len_out, len_in, h_send.at[1], h_recv.at[1], rows_x[0])

    lookup = (ids[...] == iota((ROWS, table.shape[0]), 1)).astype(BF16)
    emb[...] = mm(lookup, table[...]).astype(BF16)
    for k in range(4):
        y = (me.y + k) % 4
        args = (emb, every.at[me.role], e_send.at[k], e_recv.at[me.role],
                me.to(y_hi=y // 2, y_lo=y % 2, core=me.y_hi))
        if k:
            put(*args)
        else:
            put_or_keep(straight, *args)

    for k in range(4):
        done(by_x.at[k], x_recv.at[k])
    o, i = iota((192, 192), 0), iota((192, 192), 1)
    source = ((o % 48) // 12) * 48 + (o // 48) * 12 + o % 12
    ordered = mm((source == i).astype(BF16), by_x[...].reshape(192, OWN)).astype(BF16)

    def block(z, c):
        return w.at[pl.ds(2 * c, 2), pl.ds(pl.multiple_of(me.core * 768 + z * 48, 16), 48), :]

    for c in range(2):
        block(me.z, c)[...] = ordered[96 * c : 96 * c + 96].reshape(2, 48, OWN)

    for c in range(2):
        put(block(me.z, c), block(me.z, c), f_send.at[0, c], f_recv.at[0, c], up)
        put(block(me.z, c), block(me.z, c), b_send.at[0, c], b_recv.at[0, c], down)
        put(block(me.z, c), block(me.z, c), c_send, c_recv, other)
    for t in range(1, 9):
        fz, bz = (me.z + 16 - t) % 16, (me.z + t) % 16
        for c in range(2):
            for z, send, recv, to, last in ((fz, f_send, f_recv, up, 0), (bz, b_send, b_recv, down, 1)):
                if t == 8 and c != last:
                    continue
                done(block(z, c), recv.at[t - 1, c])
                if t < 7 or (t == 7 and c == last):
                    put(block(z, c), block(z, c), send.at[t, c], recv.at[t, c], to)
                put(block(z, c), block(z, c), c_send, c_recv, other)

    for k in range(4):
        done(every.at[k], e_recv.at[k])
    normed = norm_rows(every[...].reshape(4 * ROWS, D).astype(F32), gain[...])
    done(events, h_recv.at[0])
    done(len_in, h_recv.at[1])
    half = w.at[:, pl.ds(pl.multiple_of((1 - me.core) * 768, 16), 768), :]
    done(half, c_recv)

    keys = mm(events[...], w[0]).astype(BF16)
    values = mm(events[...], w[1]).astype(BF16)
    queries = mm(normed, w[2]).astype(BF16)
    visible = iota((128, 128), 1) < len_in[0:1, :]
    low = iota((128, 128), 1) < HEAD
    mixed = []
    for pair in range(OWN // 128):
        cut = slice(128 * pair, 128 * pair + 128)
        q, k, v = queries[:, cut], keys[:, cut], values[:, cut]
        outs = []
        for mask in (low, jnp.logical_not(low)):
            scores = mm_nt(jnp.where(mask, q, jnp.zeros_like(q)), k) * HEAD ** -0.5
            scores = jnp.where(visible, scores, -1e30)
            weights = jnp.exp(scores - jnp.max(scores, axis=-1, keepdims=True))
            probs = (weights / jnp.sum(weights, axis=-1, keepdims=True)).astype(BF16)
            outs.append(mm(probs, v))
        mixed.append(jnp.where(low, outs[0], outs[1]).astype(BF16))
    mixed = jnp.concatenate(mixed, axis=1)
    part[...] = mm_nt(mixed, w[3]).astype(BF16).reshape(4, ROWS, D)

    for level in range(4):
        own = jnp.logical_and(straight, me.role == level)
        put_or_keep(own, part.at[level], parts.at[me.y], r_send.at[level], r_recv.at[me.y],
                    me.to(y_hi=me.core, y_lo=level // 2, core=level % 2))
    total = jnp.zeros((ROWS, D), F32)
    for k in range(4):
        done(parts.at[k], r_recv.at[k])
    for k in range(4):
        total += parts[k].astype(F32)
    hidden[...] = (emb[...].astype(F32) + total).astype(BF16)

    for k in range(4):
        if k:
            done(piece, x_send.at[k])
            done(emb, e_send.at[k])
        else:
            done_unless(straight, piece, x_send.at[k])
            done_unless(straight, emb, e_send.at[k])
        own = jnp.logical_and(straight, me.role == k)
        done_unless(own, part.at[k], r_send.at[k])
    done_unless(straight, events, h_send.at[0])
    done_unless(straight, len_out, h_send.at[1])
    for t in range(8):
        for c in range(2):
            if t < 7 or c == 0:
                done(block(me.z, c), f_send.at[t, c])
            if t < 7 or c == 1:
                done(block(me.z, c), b_send.at[t, c])
    done(half, c_send)


def expert_kernel(
    hid, routes, routes_t, gain, router, wg_hbm, wu_hbm, wd_hbm,
    out,
    wg, wu, wd, packed, got_y, sorted_z, rows, res, sums, z_out, z_in, done_rows, back_z, sorted_y, back_y,
    w_sem, y_send, y_recv, z_send, z_recv, p_send, p_recv, x_send, x_recv, s_send, s_recv,
    q_send, q_recv, bz_send, bz_recv, by_send, by_recv,
):
    me = Here()
    col = me.y_lo * 4 + me.core * 2 + me.y_hi
    zp, z_lo = me.z // 2, me.z % 2

    def in_column(d):
        return me.to(y_lo=d // 4, core=(d // 2) % 2, y_hi=d % 2)

    def in_z(p):
        return me.to(z=p * 2 + z_lo)

    mate = me.to(z=zp * 2 + 1 - z_lo)
    x_of = [(me.x + k) % 4 for k in range(4)]
    greet([in_column((col + k) % 8) for k in range(1, 8)]
          + [in_z((zp + k) % 8) for k in range(1, 8)]
          + [mate] + [me.to(x=x_of[k]) for k in range(1, 4)])

    for k, (src, dst) in enumerate(((wg_hbm, wg), (wu_hbm, wu), (wd_hbm, wd))):
        pltpu.make_async_copy(src, dst, w_sem.at[k]).start()

    hidden = hid[...].astype(F32)
    moe_in = norm_rows(hidden, gain[...])

    def slots(shape, dim):
        slot = iota(shape, dim)
        return (slot // 16) * 8 + slot % 8, (slot // 8) % 2

    expert, order = slots((128, ROWS), 0)
    named = jnp.logical_or(routes_t[0:1, :] == expert, routes_t[1:2, :] == expert)
    earlier = (iota((ROWS, ROWS), 0) < iota((ROWS, ROWS), 1)).astype(BF16)
    before = mm(named.astype(BF16), earlier)
    placing = jnp.logical_and(named, before == order.astype(F32)).astype(BF16)
    packed[...] = mm(placing, moe_in).astype(BF16)

    def cut(ref, k):
        return ref.at[pl.ds(pl.multiple_of(k * 16, 16), 16), :]

    pltpu.make_async_copy(cut(packed, col), cut(got_y, col), y_recv.at[col]).start()
    for k in range(1, 8):
        d = (col + k) % 8
        put(cut(packed, d), cut(got_y, col), y_send.at[k], y_recv.at[col], in_column(d))
    for k in range(8):
        done(cut(got_y, k), y_recv.at[k])
    o, i = iota((128, 128), 0), iota((128, 128), 1)
    source = ((o // 2) % 8) * 16 + (o % 2) * 8 + o // 16
    sorted_z[...] = mm((source == i).astype(BF16), got_y[...]).astype(BF16)

    mine = rows.at[me.x, z_lo]
    pltpu.make_async_copy(cut(sorted_z, zp), cut(mine, zp), z_recv.at[zp]).start()
    for k in (4, 3, 5, 2, 6, 1, 7):
        p = (zp + k) % 8
        put(cut(sorted_z, p), cut(mine, zp), z_send.at[k], z_recv.at[zp], in_z(p))

    logits = mm(moe_in, router[...])
    lanes = iota(logits.shape, 1)
    picked = [
        jnp.sum(jnp.where(routes[:, k : k + 1] == lanes, logits, 0.0), axis=-1, keepdims=True)
        for k in range(2)
    ]
    top = jnp.maximum(picked[0], picked[1])
    powers = [jnp.exp(p - top) for p in picked]
    gates = [p / (powers[0] + powers[1]) for p in powers]
    expert_l, order_l = slots((ROWS, 128), 1)
    member = [routes[:, k : k + 1] == expert_l for k in range(2)]
    later = (iota((ROWS, ROWS), 1) < iota((ROWS, ROWS), 0)).astype(BF16)
    before_l = mm(later, jnp.logical_or(member[0], member[1]).astype(BF16))
    taking = [jnp.logical_and(m, before_l == order_l.astype(F32)).astype(BF16) for m in member]

    for k in range(8):
        done(cut(mine, k), z_recv.at[k])
    put(mine, mine, p_send, p_recv, mate)
    done(rows.at[me.x, 1 - z_lo], p_recv)
    for k in (2, 1, 3):
        put(rows.at[me.x], rows.at[me.x], x_send.at[k], x_recv.at[me.x], me.to(x=x_of[k]))

    for k, dst in enumerate((wg, wu, wd)):
        done(dst, w_sem.at[k])

    def apply(x):
        here = rows[x].reshape(256, D)
        gate, up = mm(here, wg[...]), mm(here, wu[...])
        inner = (gate / (1.0 + jnp.exp(-gate)) * up).astype(BF16)
        res[x] = mm(inner, wd[...]).astype(BF16).reshape(2, 128, D)

    apply(me.x)
    for k in (1, 3, 2):
        x = x_of[k]
        done(rows.at[x], x_recv.at[x])
        apply(x)
        put(res.at[x], sums.at[me.x], s_send.at[k], s_recv.at[me.x], me.to(x=x))
    for k in range(1, 4):
        done(sums.at[x_of[k]], s_recv.at[x_of[k]])

    def total(z):
        value = res[me.x, z].astype(F32)
        for k in range(1, 4):
            value += sums[x_of[k], z].astype(F32)
        return value

    z_out[...] = total(1 - z_lo).astype(BF16)
    put(z_out, z_in, q_send, q_recv, mate)
    own = total(z_lo)
    done(z_in, q_recv)
    done_rows[...] = (own + z_in[...].astype(F32)).astype(BF16)

    pltpu.make_async_copy(cut(done_rows, zp), cut(back_z, zp), bz_recv.at[zp]).start()
    for k in (4, 3, 5, 2, 6, 1, 7):
        p = (zp + k) % 8
        put(cut(done_rows, p), cut(back_z, zp), bz_send.at[k], bz_recv.at[zp], in_z(p))
    for k in range(8):
        done(cut(back_z, k), bz_recv.at[k])
    source = (o % 8) * 16 + (o // 16) * 2 + (o // 8) % 2
    sorted_y[...] = mm((source == i).astype(BF16), back_z[...]).astype(BF16)
    pltpu.make_async_copy(cut(sorted_y, col), cut(back_y, col), by_recv.at[col]).start()
    for k in range(1, 8):
        d = (col + k) % 8
        put(cut(sorted_y, d), cut(back_y, col), by_send.at[k], by_recv.at[col], in_column(d))
    for k in range(8):
        done(cut(back_y, k), by_recv.at[k])

    mixed = gates[0] * mm(taking[0], back_y[...]) + gates[1] * mm(taking[1], back_y[...])
    out[...] = (hidden + mixed).astype(BF16)

    for k in range(1, 8):
        for ref, sem in ((packed, y_send), (sorted_z, z_send), (done_rows, bz_send), (sorted_y, by_send)):
            done(cut(ref, 0), sem.at[k])
    done(mine, p_send)
    for k in range(1, 4):
        done(rows.at[me.x], x_send.at[k])
        done(res.at[me.x], s_send.at[k])
    done(z_out, q_send)


def dma(*shape):
    return pltpu.SemaphoreType.DMA(shape)


def vmem(*shape, dtype=BF16):
    return pltpu.VMEM(shape, dtype)


VM = pl.BlockSpec(memory_space=pltpu.VMEM)
SM = pl.BlockSpec(memory_space=pltpu.SMEM)
ANY = pl.BlockSpec(memory_space=pl.ANY)


def shards(history, lengths, beam_ids, routes, code_table, w_key, w_value, w_query, w_out,
           norm_gain, moe_gain, w_router, w_gate, w_up, w_down):
    piece = jnp.concatenate([w_key, w_value, w_query, w_out.T], axis=0)
    hidden = pl.pallas_call(
        attend_kernel,
        out_shape=jax.ShapeDtypeStruct((ROWS, D), BF16),
        in_specs=[VM, SM, VM, VM, VM, ANY],
        out_specs=VM,
        scratch_shapes=[
            vmem(ROWS, D), vmem(4, ROWS, D), vmem(128, D), vmem(8, 128, dtype=I32), vmem(8, 128, dtype=I32),
            vmem(4, 48, OWN), vmem(4, D, OWN), vmem(4, ROWS, D), vmem(4, ROWS, D),
            dma(4), dma(4), dma(4), dma(4), dma(2), dma(2), dma(8, 2), dma(8, 2), dma(8, 2), dma(8, 2),
            pltpu.SemaphoreType.DMA, pltpu.SemaphoreType.DMA, dma(4), dma(4),
        ],
        compiler_params=pltpu.CompilerParams(
            collective_id=0, has_side_effects=True, vmem_limit_bytes=48 * 1024 * 1024
        ),
        name="attend",
    )(beam_ids.reshape(ROWS, 1), lengths, norm_gain.reshape(1, D), piece, code_table, history.reshape(128, D))
    pairs = routes.reshape(ROWS, 2)
    result = pl.pallas_call(
        expert_kernel,
        out_shape=jax.ShapeDtypeStruct((ROWS, D), BF16),
        in_specs=[VM] * 5 + [ANY] * 3,
        out_specs=VM,
        scratch_shapes=[
            vmem(D, OWN), vmem(D, OWN), vmem(OWN, D), vmem(128, D), vmem(128, D), vmem(128, D),
            vmem(4, 2, 128, D), vmem(4, 2, 128, D), vmem(4, 2, 128, D), vmem(128, D), vmem(128, D),
            vmem(128, D), vmem(128, D), vmem(128, D), vmem(128, D),
            dma(3), dma(8), dma(8), dma(8), dma(8),
            pltpu.SemaphoreType.DMA, pltpu.SemaphoreType.DMA, dma(4), dma(4), dma(4), dma(4),
            pltpu.SemaphoreType.DMA, pltpu.SemaphoreType.DMA, dma(8), dma(8), dma(8), dma(8),
        ],
        compiler_params=pltpu.CompilerParams(
            collective_id=1, has_side_effects=True, vmem_limit_bytes=48 * 1024 * 1024
        ),
        name="experts",
    )(hidden, pairs, pairs.T, moe_gain.reshape(1, D), w_router, w_gate[0], w_up[0], w_down[0])
    return result.reshape(1, 1, ROWS, D)


def solution(mesh):
    return jax.shard_map(
        shards,
        mesh=mesh,
        in_specs=(
            P("shard", None, None),
            P("shard"),
            P("shard", "role", None),
            P("shard", "role", None, None),
            P("role", None),
            P("shard", "role"),
            P("shard", "role"),
            P("shard", "role"),
            P("role", "shard"),
            P(),
            P(),
            P(),
            P(("role", "shard"), None, None),
            P(("role", "shard"), None, None),
            P(("role", "shard"), None, None),
        ),
        out_specs=P("shard", "role", None, None),
        check_vma=False,
    )
```

time: 1290 us -> 227 us (0.18)
  waiting for transfers between devices: 934 us -> 0 us
  blocking collectives: 258 us -> 0 us
  Pallas kernels: 0 us -> 216 us
  local copies, waits for them, and re-layouts: 41.8 us -> 8.43 us
  matrix products: 19.1 us -> 0 us
  between operations: 14.1 us -> 0.82 us
    all_gather x4 -> x0, waiting for transfers between devices: 759 us -> none  [the longest x1 193 us: shards(): lax.all_gather(w_query, 'shard', axis=0, tiled=True)]
    all_to_all x3 -> x0, blocking collectives: 246 us -> none  [the longest x1 163 us: shards(): lax.all_to_all(lax.all_to_all(outgoing, 'role', split_axis=0, concat_axis...]
    pallas_call x0 -> x2, Pallas kernels: none -> 216 us  [the longest x1 151 us: shards(): pl.pallas_call(expert_kernel, out_shape=jax.ShapeDtypeStruct((ROWS, D), B...]
    all_to_all x1 -> x0, waiting for transfers between devices: 144 us -> none  [shards(): lax.all_to_all(lax.all_to_all(result_rows.reshape(arrived.shape), 'role',...]
    reduce_scatter x1 -> x0, waiting for transfers between devices: 29 us -> none  [shards(): lax.psum_scatter(partial_out.astype(jnp.bfloat16), 'role', scatter_dimens...]
    dot_general x12 -> x0, matrix products: 18.8 us -> none  [the longest x1 7.84 us: shards(): jnp.dot(inner, w_down[0], preferred_element_type=jnp.float32)]
    all_to_all x4 -> x0, local copies, waits for them, and re-layouts: 15.5 us -> none  [the longest x1 4.51 us: shards(): lax.all_to_all(lax.all_to_all(result_rows.reshape(arrived.shape), 'role',...]
  transfers between devices with their start and end apart: 6 -> 0, of which waited for: 6 -> 0; matrix products, arithmetic and copies ran while one was open for 1% -> 0% of each run, Pallas kernels for 0% -> 0%
where the time goes in v1:
time: 227 us; the launch traced here: 226 us
  Pallas kernels  216 us (95%)
  local copies, waits for them, and re-layouts  8.43 us (4%)
    pallas_call x1, Pallas kernels, shards(): pl.pallas_call(expert_kernel, out_shape=jax.ShapeDtypeStruct((ROWS, D), B...  151 us
    pallas_call x1, Pallas kernels, shards(): pl.pallas_call(attend_kernel, out_shape=jax.ShapeDtypeStruct((ROWS, D), B...  64.8 us
    unnamed x16, local copies, waits for them, and re-layouts  5.54 us

profile of v1, /device:TPU:1, one launch (start us, length us, event | category | flops | bytes accessed | tf_op | source)
XLA Modules:
  0.0 225.9 jit_solution(7944864375300920003)
XLA Ops:
  0.0 0.0 copy-start
  0.8 0.7 reshape.19.gain
  1.5 0.7 reshape.22.gain
  2.2 0.7 copy.16.ids
  2.9 0.8 copy.17.routes
  3.7 0.8 pad_maximum_fusion.piece
  4.4 0.0 copy-start.3
  4.4 1.1 copy-done.3
  5.6 0.0 copy-start.4
  5.6 1.0 copy-done.4
  6.6 0.0 copy-start.6
  6.6 0.0 copy-start.5
  6.6 64.8 %attend.1.hid = bf16[32,1536]{1,0:T(8,128)(2,1)S(1)} custom-call(s32[32,1]{1,0:T(8,128)S(1)} %copy.16.ids, s32[1]{0:T(128)S(6)} %copy.20.lens, f32[1,1536]{1,0:T(1,128)S(1)} %reshape.19.gain, bf16[48,384]{1,0:T(8,128)(2,1)S(1)} %pad_maximum_fusion.piece, bf16[256,1536]{1,0:T(8,128)(2,1)S(1)} %copy-done.3, bf16[128,1536]{1,0:T(8,128)(2,1)S(1)} %bitcast.13), custom_call_target="tpu_custom_call" | custom-call | tf_op jit(solution)/shard_map/attend/pallas_call | solution.py:366
  71.3 0.0 copy-done.6
  71.3 0.2 copy.18.router
  71.6 0.0 copy-done
  71.6 0.0 copy-done.5
  71.6 0.0 copy-start.1
  71.6 1.3 copy-done.1
  72.9 0.0 copy-start.2
  72.9 1.3 copy-done.2
  74.1 151.1 %experts.1 = bf16[32,1536]{1,0:T(8,128)(2,1)S(1)} custom-call(bf16[32,1536]{1,0:T(8,128)(2,1)S(1)} %attend.1.hid, s32[32,2]{1,0:T(8,128)S(1)} %copy.17.routes, s32[2,32]{1,0:T(2,128)S(1)} %bitcast.16, f32[1,1536]{1,0:T(1,128)S(1)} %reshape.22.gain, bf16[1536,64]{1,0:T(8,128)(2,1)S(1)} %copy.18.router, bf16[1536,384]{1,0:T(8,128)(2,1)S(1)} %bitcast.10, ...), custom_call_target="tpu_custom_call" | custom-call | tf_op jit(solution)/shard_map/experts/pallas_call | solution.py:383
  225.2 0.6 copy.21
Async XLA Ops:
  0.0 71.6 %copy-start = (bf16[1,1536,384]{2,1,0:T(8,128)(2,1)S(1)}, bf16[1,1536,384]{2,1,0:T(8,128)(2,1)}, u32[]{:S(2)}) copy-start(bf16[1,1536,384]{2,1,0:T(8,128)(2,1)} %param.27) | copy-start | bytes 3538948
  4.4 1.1 copy-start.3
  5.6 1.0 copy-start.4
  6.6 64.8 %copy-start.6 = (bf16[1536,64]{0,1:T(8,128)(2,1)S(1)}, bf16[1536,64]{0,1:T(8,128)(2,1)}, u32[]{:S(2)}) copy-start(bf16[1536,64]{0,1:T(8,128)(2,1)} %param.26) | copy-start | bytes 589828
  6.6 65.0 %copy-start.5 = (s32[1,1,32,2]{2,3,1,0:T(2,128)S(1)}, s32[1,1,32,2]{2,3,1,0:T(2,128)}, u32[]{:S(2)}) copy-start(s32[1,1,32,2]{2,3,1,0:T(2,128)} %param.18) | copy-start | bytes 772
  71.6 1.3 copy-start.1
  72.9 1.3 copy-start.2

commit v2 on v1

v2 whole, which is shorter than its diff:
```python
import functools

import jax
import jax.numpy as jnp
from jax import lax
from jax.experimental import pallas as pl
from jax.experimental.pallas import tpu as pltpu
from jax.sharding import PartitionSpec as P

MESH = pl.DeviceIdType.MESH
F32, BF16, I32 = jnp.float32, jnp.bfloat16, jnp.int32
D = 1536
HEAD = 64
OWN = 384
ROWS = 32
EPS = 1e-06


class Here:
    def __init__(self):
        role, shard = lax.axis_index("role"), lax.axis_index("shard")
        self.role = role
        self.y_lo, self.core = role // 2, role % 2
        self.y_hi, self.z, self.x = shard // 64, (shard // 4) % 16, shard % 4
        self.y = self.y_hi * 2 + self.y_lo

    def to(self, y_hi=None, y_lo=None, core=None, z=None, x=None):
        pick = lambda new, old: old if new is None else new
        y_hi, y_lo, core = pick(y_hi, self.y_hi), pick(y_lo, self.y_lo), pick(core, self.core)
        z, x = pick(z, self.z), pick(x, self.x)
        return (y_lo * 2 + core, y_hi * 64 + z * 4 + x)


def done(ref, sem):
    pltpu.make_async_copy(ref, ref, sem).wait()


def norm_rows(values, gain):
    power = jnp.mean(values * values, axis=-1, keepdims=True)
    return (values * lax.rsqrt(power + EPS) * gain).astype(BF16)


def mm(a, b):
    return jnp.dot(a, b, preferred_element_type=F32)


def mm_nt(a, b):
    return lax.dot_general(a, b, (((1,), (1,)), ((), ())), preferred_element_type=F32)


def iota(shape, dim):
    return lax.broadcasted_iota(I32, shape, dim)


ORDER = (1, 2, 3, 0)
CHUNKS = len(ORDER)
LEAD = 2
LAG = (2, 4)
FORWARD = (1, 2)
BACKWARD = (1, 2, 3)


def layer_kernel(
    ids, lens, routes_t, gain, moe_gain, w_key, w_value, w_query, w_out_t, router_t, table_hbm, hist,
    wg_hbm, wu_hbm, wd_hbm,
    out,
    table, emb, every, events, len_out, len_in, piece, raw, w, part, parts,
    wg, wu, wd, packed, got_y, sorted_z, rows, res, halves, sums, z_out, z_in, fin, back_z, sorted_y, back_y,
    t_sem, w_sem, m_send, m_recv, e_send, e_recv, hi_send, hi_recv, f_send, f_recv, b_send, b_recv,
    d_send, d_recv, l_send, l_recv, c_send, c_recv, o_send, o_recv,
    y_send, y_recv, z_send, z_recv, p_send, p_recv, g_send, g_recv, r_send, r_recv,
    h_send, h_recv, s_send, s_recv, q_send, q_recv, bz_send, bz_recv, by_send, by_recv,
):
    me = Here()
    sent = []

    def put(src, dst, send, recv, to, listed=True):
        pltpu.make_async_remote_copy(
            src_ref=src, dst_ref=dst, send_sem=send, recv_sem=recv, device_id=to, device_id_type=MESH
        ).start()
        if listed:
            sent.append((src, send, None))

    def put_or_keep(is_self, src, dst, send, recv, to):
        @pl.when(is_self)
        def _():
            pltpu.make_async_copy(src, dst, recv).start()

        @pl.when(jnp.logical_not(is_self))
        def _():
            put(src, dst, send, recv, to, listed=False)

        sent.append((src, send, is_self))

    def all_left():
        for src, send, is_self in sent:
            if is_self is None:
                done(src, send)
            else:
                pl.when(jnp.logical_not(is_self))(functools.partial(done, src, send))

    straight = me.y_hi == me.core
    zp, z_lo = me.z // 2, me.z % 2
    col = me.y_lo * 4 + me.core * 2 + me.y_hi

    def in_column(d):
        return me.to(y_lo=d // 4, core=(d // 2) % 2, y_hi=d % 2)

    mirrored = [me.to(y_hi=me.core, core=me.y_hi, x=(me.x + k) % 4) for k in range(4)]
    other = me.to(core=1 - me.core)
    z_up, z_down = me.to(z=(me.z + 1) % 16), me.to(z=(me.z + 15) % 16)
    mate = me.to(z=zp * 2 + 1 - z_lo)
    x_up, x_far, x_down = [(me.x + k) % 4 for k in (1, 2, 3)]
    up, down = me.to(x=x_up), me.to(x=x_down)
    partners = ([in_column((col + k) % 8) for k in range(1, 8)] + mirrored[1:] + [z_up, z_down]
                + [me.to(z=(me.z + k) % 16) for k in range(2, 15)] + [up, down])
    barrier = pltpu.get_barrier_semaphore()
    for to in partners:
        pl.semaphore_signal(barrier, inc=1, device_id=to, device_id_type=MESH)

    pltpu.make_async_copy(table_hbm, table, t_sem).start()
    for k, (src, dst) in enumerate(((wg_hbm, wg), (wu_hbm, wu), (wd_hbm, wd))):
        pltpu.make_async_copy(src, dst, w_sem.at[k]).start()

    o, i = iota((48, 12), 0), iota((48, 12), 1)
    stacked = jnp.zeros((48, OWN), F32)
    for m, ref in enumerate((w_key, w_value, w_query, w_out_t)):
        stacked += mm((o == i + 12 * m).astype(BF16), ref[...])
    piece[...] = stacked.astype(BF16)
    len_out[...] = jnp.full((8, 128), lens[0], I32)
    eye = (iota((ROWS, ROWS), 0) == iota((ROWS, ROWS), 1)).astype(BF16)
    lookup = mm_nt(eye, (iota((256, ROWS), 0) == ids[...]).astype(BF16)).astype(BF16)
    done(table, t_sem)
    emb[...] = mm(lookup, table[...]).astype(BF16)

    pl.semaphore_wait(barrier, len(partners))

    put_or_keep(straight, piece, raw.at[me.x, me.z], m_send, m_recv, mirrored[0])

    o, i = iota((192, 192), 0), iota((192, 192), 1)
    ordering = (((o % 48) // 12) * 48 + (o // 48) * 12 + o % 12 == i).astype(BF16)

    def block(z):
        return w.at[:, pl.ds(pl.multiple_of(me.core * 768 + z * 48, 16), 48), :]

    def z_of(n):
        return (me.z + 16 - n) % 16 if n < 8 else (me.z + n - 7) % 16

    def share(n):
        mine = raw.at[me.x, z_of(n)]
        put(mine, mine, d_send.at[n, 0], d_recv.at[n, 0], up)
        put(mine, mine, d_send.at[n, 1], d_recv.at[n, 1], down)

    def pass_on(n):
        z = z_of(n)
        low, high = raw.at[x_down, z], raw.at[x_up, z]
        done(low, d_recv.at[n, 0])
        if n < 8:
            put(low, low, l_send.at[n], l_recv.at[n], up)
        done(high, d_recv.at[n, 1])
        if n >= 8:
            put(high, high, l_send.at[n], l_recv.at[n], down)

    def settle(n):
        z = z_of(n)
        done(raw.at[x_far, z], l_recv.at[n])
        pieces = jnp.concatenate([raw[x, z] for x in range(4)], axis=0)
        block(z)[...] = mm(ordering, pieces).astype(BF16).reshape(4, 48, OWN)
        put(block(z), block(z), c_send.at[n], c_recv, other)

    own_piece = raw.at[me.x, me.z]
    done(own_piece, m_recv)
    put(own_piece, own_piece, f_send.at[0], f_recv.at[0], z_up)
    put(own_piece, own_piece, b_send.at[0], b_recv.at[0], z_down)
    share(0)

    for k in range(4):
        y = (me.y + k) % 4
        args = (emb, every.at[me.role], e_send.at[k], e_recv.at[me.role],
                me.to(y_hi=y // 2, y_lo=y % 2, core=me.y_hi))
        if k:
            put(*args)
        else:
            put_or_keep(straight, *args)

    put_or_keep(straight, hist, events, hi_send.at[0], hi_recv.at[0], mirrored[0])
    put_or_keep(straight, len_out, len_in, hi_send.at[1], hi_recv.at[1], mirrored[0])

    def slots(shape, dim):
        slot = iota(shape, dim)
        return (slot // 16) * 8 + slot % 8, (slot // 8) % 2

    routes = mm_nt(eye, routes_t[...].astype(BF16)).astype(I32)
    expert, order = slots((128, ROWS), 0)
    named = jnp.logical_or(routes_t[0:1, :] == expert, routes_t[1:2, :] == expert)
    earlier = (iota((ROWS, ROWS), 0) < iota((ROWS, ROWS), 1)).astype(BF16)
    before = mm(named.astype(BF16), earlier)
    placing = jnp.logical_and(named, before == order.astype(F32)).astype(BF16)
    expert_l, order_l = slots((ROWS, 128), 1)
    member = [routes[:, k : k + 1] == expert_l for k in range(2)]
    later = (iota((ROWS, ROWS), 1) < iota((ROWS, ROWS), 0)).astype(BF16)
    before_l = mm(later, jnp.logical_or(member[0], member[1]).astype(BF16))
    taking = [jnp.logical_and(m, before_l == order_l.astype(F32)).astype(BF16) for m in member]

    def lagging(stage, t):
        if t == 0:
            stage(0)
        elif 0 < t < 8:
            stage(t)
            stage(t + 7)
        elif t == 8:
            stage(15)

    for t in range(1, 9 + LAG[1]):
        if t < 9:
            for n, send, recv, to in ((t, f_send, f_recv, z_up), (t + 7, b_send, b_recv, z_down)):
                if t == 8 and n == 8:
                    continue
                ref = raw.at[me.x, z_of(n)]
                done(ref, recv.at[t - 1])
                if t < 7 or (t == 7 and n == 14):
                    put(ref, ref, send.at[t], recv.at[t], to)
                share(n)
        lagging(pass_on, t - LAG[0])
        lagging(settle, t - LAG[1])

    for k in range(4):
        done(every.at[k], e_recv.at[k])
    normed = norm_rows(every[...].reshape(4 * ROWS, D).astype(F32), gain[...].reshape(1, D))
    done(events, hi_recv.at[0])
    done(len_in, hi_recv.at[1])
    half = w.at[:, pl.ds(pl.multiple_of((1 - me.core) * 768, 16), 768), :]
    done(half, c_recv)

    keys = mm(events[...], w[0]).astype(BF16)
    values = mm(events[...], w[1]).astype(BF16)
    queries = mm(normed, w[2]).astype(BF16)
    visible = iota((128, 128), 1) < len_in[0:1, :]
    low = iota((128, 128), 1) < HEAD
    mixed = []
    for pair in range(OWN // 128):
        cols = slice(128 * pair, 128 * pair + 128)
        q, k, v = queries[:, cols], keys[:, cols], values[:, cols]
        outs = []
        for mask in (low, jnp.logical_not(low)):
            scores = mm_nt(jnp.where(mask, q, jnp.zeros_like(q)), k) * HEAD ** -0.5
            scores = jnp.where(visible, scores, -1e30)
            weights = jnp.exp(scores - jnp.max(scores, axis=-1, keepdims=True))
            probs = (weights / jnp.sum(weights, axis=-1, keepdims=True)).astype(BF16)
            outs.append(mm(probs, v))
        mixed.append(jnp.where(low, outs[0], outs[1]).astype(BF16))
    mixed = jnp.concatenate(mixed, axis=1)
    part[...] = mm_nt(mixed, w[3]).astype(BF16).reshape(4, ROWS, D)

    for level in range(4):
        own = jnp.logical_and(straight, me.role == level)
        put_or_keep(own, part.at[level], parts.at[me.y], o_send.at[level], o_recv.at[me.y],
                    me.to(y_hi=me.core, y_lo=level // 2, core=level % 2))
    for k in range(4):
        done(parts.at[k], o_recv.at[k])
    attended = parts[0].astype(F32) + parts[1].astype(F32) + parts[2].astype(F32) + parts[3].astype(F32)
    hidden = (emb[...].astype(F32) + attended).astype(BF16).astype(F32)
    moe_in = norm_rows(hidden, moe_gain[...].reshape(1, D))
    packed[...] = mm(placing, moe_in).astype(BF16)

    def cut(ref, k):
        return ref.at[pl.ds(pl.multiple_of(k * 16, 16), 16), :]

    pltpu.make_async_copy(cut(packed, col), cut(got_y, col), y_recv.at[col]).start()
    for k in range(1, 8):
        d = (col + k) % 8
        put(cut(packed, d), cut(got_y, col), y_send.at[k], y_recv.at[col], in_column(d))

    logits = mm_nt(moe_in, router_t[...])
    lanes = iota(logits.shape, 1)
    picked = [
        jnp.sum(jnp.where(routes[:, k : k + 1] == lanes, logits, 0.0), axis=-1, keepdims=True)
        for k in range(2)
    ]
    top = jnp.maximum(picked[0], picked[1])
    powers = [jnp.exp(p - top) for p in picked]
    gates = [p / (powers[0] + powers[1]) for p in powers]

    for k in range(8):
        done(cut(got_y, k), y_recv.at[k])
    o, i = iota((128, 128), 0), iota((128, 128), 1)
    source = ((o // 2) % 8) * 16 + (o % 2) * 8 + o // 16
    sorted_z[...] = mm((source == i).astype(BF16), got_y[...]).astype(BF16)

    def pair_below(n, z):
        return (zp + 8 - n + 2 * n * z) % 8

    def send_z(n):
        if n:
            for first, p in ((0, (zp + n) % 8), (1, (zp + 8 - n) % 8)):
                put(cut(sorted_z, p), rows.at[n, me.x, first, pl.ds(16 * z_lo, 16), :],
                    z_send.at[n, first], z_recv.at[n, z_lo], me.to(z=p * 2 + first))
        else:
            p = (zp + 4) % 8
            put(cut(sorted_z, p), rows.at[0, me.x, 1 - z_lo, pl.ds(16, 16), :],
                z_send.at[0, 1], z_recv.at[0, 1], me.to(z=p * 2 + 1 - z_lo))
            pltpu.make_async_copy(
                cut(sorted_z, zp), rows.at[0, me.x, z_lo, pl.ds(0, 16), :], z_recv.at[0, 0]).start()

    def share_own(n):
        mine = rows.at[n, me.x, z_lo]
        for h in range(2):
            done(rows.at[n, me.x, z_lo, pl.ds(16 * h, 16), :], z_recv.at[n, h])
        put(mine, mine, p_send.at[n], p_recv.at[n], mate)
        put(mine, mine, g_send.at[n, 0, z_lo], g_recv.at[n, 0, z_lo], up)
        put(mine, mine, g_send.at[n, 1, z_lo], g_recv.at[n, 1, z_lo], down)

    def share_mate(n):
        theirs = rows.at[n, me.x, 1 - z_lo]
        done(theirs, p_recv.at[n])
        put(theirs, theirs, g_send.at[n, 0, 1 - z_lo], g_recv.at[n, 0, 1 - z_lo], up)
        put(theirs, theirs, g_send.at[n, 1, 1 - z_lo], g_recv.at[n, 1, 1 - z_lo], down)

    def relay(n):
        first, second = rows.at[n, x_down, 0], rows.at[n, x_up, 1]
        done(first, g_recv.at[n, 0, 0])
        put(first, first, r_send.at[n, 0], r_recv.at[n, 0], up)
        done(second, g_recv.at[n, 1, 1])
        put(second, second, r_send.at[n, 1], r_recv.at[n, 1], down)
        done(rows.at[n, x_down, 1], g_recv.at[n, 0, 1])
        done(rows.at[n, x_up, 0], g_recv.at[n, 1, 0])

    def apply(n):
        for b in range(2):
            done(rows.at[n, x_far, b], r_recv.at[n, b])
        if n == ORDER[0]:
            for k, dst in enumerate((wg, wu, wd)):
                done(dst, w_sem.at[k])
        here = rows[n].reshape(256, D)
        gate, lift = mm(here, wg[...]), mm(here, wu[...])
        inner = (gate / (1.0 + jnp.exp(-gate)) * lift).astype(BF16)
        res[n] = mm(inner, wd[...]).astype(BF16).reshape(4, 2, 32, D)
        put(res.at[n, x_far, 0], halves.at[n, 0], h_send.at[n, 0], h_recv.at[n, 0], up)
        put(res.at[n, x_far, 1], halves.at[n, 1], h_send.at[n, 1], h_recv.at[n, 1], down)

    def add_halves(n):
        for b, x, to in ((0, x_up, up), (1, x_down, down)):
            done(halves.at[n, b], h_recv.at[n, b])
            res[n, x, b] = (res[n, x, b].astype(F32) + halves[n, b].astype(F32)).astype(BF16)
            put(res.at[n, x], sums.at[n, b], s_send.at[n, b], s_recv.at[n, b], to)

    def total(n, z):
        return res[n, me.x, z].astype(F32) + sums[n, 0, z].astype(F32) + sums[n, 1, z].astype(F32)

    def add_x(n):
        for b in range(2):
            done(sums.at[n, b], s_recv.at[n, b])
        z_out[n] = total(n, 1 - z_lo).astype(BF16)
        put(z_out.at[n], z_in.at[n], q_send.at[n], q_recv.at[n], mate)

    def add_mate(n):
        done(z_in.at[n], q_recv.at[n])
        fin[n] = (total(n, z_lo) + z_in[n].astype(F32)).astype(BF16)
        halves_of = [fin.at[n, pl.ds(16 * h, 16), :] for h in range(2)]
        if n:
            p = pair_below(n, z_lo)
            for h in range(2):
                put(halves_of[h], cut(back_z, zp), bz_send.at[n, h], bz_recv.at[n, z_lo], me.to(z=p * 2 + h))
        else:
            pltpu.make_async_copy(halves_of[0], cut(back_z, zp), bz_recv.at[0, 0]).start()
            p = (zp + 4) % 8
            put(halves_of[1], cut(back_z, zp), bz_send.at[0, 1], bz_recv.at[0, 1], me.to(z=p * 2 + 1 - z_lo))

    def run(stages):
        for tick in range(CHUNKS + max(begin for _, begin in stages)):
            for stage, begin in stages:
                if 0 <= tick - begin < CHUNKS:
                    stage(ORDER[tick - begin])

    run(((send_z, 0), (share_own, LEAD), (share_mate, LEAD + FORWARD[0]), (relay, LEAD + FORWARD[1])))
    run(((apply, 0), (add_halves, BACKWARD[0]), (add_x, BACKWARD[1]), (add_mate, BACKWARD[2])))

    for n in range(CHUNKS):
        if n:
            done(cut(back_z, (zp + n) % 8), bz_recv.at[n, 0])
            done(cut(back_z, (zp + 8 - n) % 8), bz_recv.at[n, 1])
        else:
            done(cut(back_z, zp), bz_recv.at[0, 0])
            done(cut(back_z, (zp + 4) % 8), bz_recv.at[0, 1])
    source = (o % 8) * 16 + (o // 16) * 2 + (o // 8) % 2
    sorted_y[...] = mm((source == i).astype(BF16), back_z[...]).astype(BF16)
    pltpu.make_async_copy(cut(sorted_y, col), cut(back_y, col), by_recv.at[col]).start()
    for k in range(1, 8):
        d = (col + k) % 8
        put(cut(sorted_y, d), cut(back_y, col), by_send.at[k], by_recv.at[col], in_column(d))
    for k in range(8):
        done(cut(back_y, k), by_recv.at[k])

    chosen = gates[0] * mm(taking[0], back_y[...]) + gates[1] * mm(taking[1], back_y[...])
    out[...] = (hidden + chosen).astype(BF16)

    all_left()


def dma(*shape):
    return pltpu.SemaphoreType.DMA(shape)


def vmem(*shape, dtype=BF16):
    return pltpu.VMEM(shape, dtype)


VM = pl.BlockSpec(memory_space=pltpu.VMEM)
SM = pl.BlockSpec(memory_space=pltpu.SMEM)
HB = pl.BlockSpec(memory_space=pltpu.HBM)
ONE = pltpu.SemaphoreType.DMA


def shards(history, lengths, beam_ids, routes, code_table, w_key, w_value, w_query, w_out,
           norm_gain, moe_gain, w_router, w_gate, w_up, w_down):
    n = CHUNKS
    result = pl.pallas_call(
        layer_kernel,
        out_shape=jax.ShapeDtypeStruct((ROWS, D), BF16),
        in_specs=[VM, SM] + [VM] * 8 + [HB] * 5,
        out_specs=VM,
        scratch_shapes=[
            vmem(256, D), vmem(ROWS, D), vmem(4, ROWS, D), vmem(128, D),
            vmem(8, 128, dtype=I32), vmem(8, 128, dtype=I32),
            vmem(48, OWN), vmem(4, 16, 48, OWN), vmem(4, D, OWN), vmem(4, ROWS, D), vmem(4, ROWS, D),
            vmem(D, OWN), vmem(D, OWN), vmem(OWN, D), vmem(128, D), vmem(128, D), vmem(128, D),
            vmem(n, 4, 2, 32, D), vmem(n, 4, 2, 32, D), vmem(n, 2, 32, D), vmem(n, 2, 2, 32, D),
            vmem(n, 32, D), vmem(n, 32, D), vmem(n, 32, D), vmem(128, D), vmem(128, D), vmem(128, D),
            ONE, dma(3), ONE, ONE, dma(4), dma(4), dma(2), dma(2),
            dma(8), dma(8), dma(8), dma(8), dma(16, 2), dma(16, 2), dma(16), dma(16), dma(16), ONE, dma(4), dma(4),
            dma(8), dma(8), dma(n, 2), dma(n, 2), dma(n), dma(n), dma(n, 2, 2), dma(n, 2, 2), dma(n, 2), dma(n, 2),
            dma(n, 2), dma(n, 2), dma(n, 2), dma(n, 2), dma(n), dma(n), dma(n, 2), dma(n, 2), dma(8), dma(8),
        ],
        compiler_params=pltpu.CompilerParams(
            collective_id=0, has_side_effects=True, vmem_limit_bytes=56 * 1024 * 1024
        ),
        name="layer",
    )(beam_ids.reshape(1, ROWS), lengths, routes.reshape(ROWS, 2).T, norm_gain, moe_gain,
      w_key, w_value, w_query, w_out.T, w_router.T, code_table, history[0], w_gate[0], w_up[0], w_down[0])
    return result.reshape(1, 1, ROWS, D)


def solution(mesh):
    return jax.shard_map(
        shards,
        mesh=mesh,
        in_specs=(
            P("shard", None, None),
            P("shard"),
            P("shard", "role", None),
            P("shard", "role", None, None),
            P("role", None),
            P("shard", "role"),
            P("shard", "role"),
            P("shard", "role"),
            P("role", "shard"),
            P(),
            P(),
            P(),
            P(("role", "shard"), None, None),
            P(("role", "shard"), None, None),
            P(("role", "shard"), None, None),
        ),
        out_specs=P("shard", "role", None, None),
        check_vma=False,
    )
```

time: 227 us -> 163 us (0.72)
  Pallas kernels: 216 us -> 160 us
  local copies, waits for them, and re-layouts: 8.43 us -> 1.54 us
    pallas_call x2 -> x1, Pallas kernels: 216 us -> 160 us  [shards(): pl.pallas_call(layer_kernel, out_shape=jax.ShapeDtypeStruct((ROWS, D), BF...]
    unnamed x16 -> x1, local copies, waits for them, and re-layouts: 5.54 us -> 1.54 us
    reshape x4 -> x0, local copies, waits for them, and re-layouts: 2.9 us -> none  [the longest x1 0.76 us: shards(): pairs = routes.reshape(ROWS, 2)]
where the time goes in v2:
time: 163 us
  Pallas kernels  160 us (98%)
    pallas_call x1, Pallas kernels, shards(): pl.pallas_call(layer_kernel, out_shape=jax.ShapeDtypeStruct((ROWS, D), BF...  160 us

profile of v2, /device:TPU:1, one launch (start us, length us, event | category | flops | bytes accessed | tf_op | source)
XLA Modules:
  0.0 162.6 jit_solution(750480985121008930)
XLA Ops:
  0.7 160.4 %layer.1 = bf16[32,1536]{1,0:T(8,128)(2,1)} custom-call(s32[1,32]{1,0:T(1,128)} %bitcast.19, s32[1]{0:T(128)S(6)} %copy.17.lens, s32[2,32]{1,0:T(2,128)} %bitcast.18, f32[1536]{0:T(1024)} %gain.1, f32[1536]{0:T(1024)} %moe_gain.1, bf16[12,384]{1,0:T(8,128)(2,1)} %w_key.1, bf16[12,384]{1,0:T(8,128)(2,1)} %w_value.1, bf16[12,384]{1,0:T(8,128)(2,1)} %w_query.1, ...), custom_call_target="tpu_custom_call" | custom-call | tf_op jit(solution)/shard_map/layer/pallas_call | solution.py:417
  161.1 1.5 copy.18

commit v3 on v2

--- a/solution.py
+++ b/solution.py
@@ -52,12 +52,12 @@
     return lax.broadcasted_iota(I32, shape, dim)
 
 
-ORDER = (1, 2, 3, 0)
+ORDER = (0, 2, 4, 5, 6, 1, 7, 3)
+Z_ORDER = (1, 2, 0, 3)
 CHUNKS = len(ORDER)
-LEAD = 2
+BEGIN = (0, 1, 2, 3, 4, 5, 6)
 LAG = (2, 4)
-FORWARD = (1, 2)
-BACKWARD = (1, 2, 3)
+DIRECT_FROM = 6
 
 
 def layer_kernel(
@@ -106,14 +106,13 @@
     def in_column(d):
         return me.to(y_lo=d // 4, core=(d // 2) % 2, y_hi=d % 2)
 
-    mirrored = [me.to(y_hi=me.core, core=me.y_hi, x=(me.x + k) % 4) for k in range(4)]
+    mirror = me.to(y_hi=me.core, core=me.y_hi)
     other = me.to(core=1 - me.core)
     z_up, z_down = me.to(z=(me.z + 1) % 16), me.to(z=(me.z + 15) % 16)
     mate = me.to(z=zp * 2 + 1 - z_lo)
     x_up, x_far, x_down = [(me.x + k) % 4 for k in (1, 2, 3)]
-    up, down = me.to(x=x_up), me.to(x=x_down)
-    partners = ([in_column((col + k) % 8) for k in range(1, 8)] + mirrored[1:] + [z_up, z_down]
-                + [me.to(z=(me.z + k) % 16) for k in range(2, 15)] + [up, down])
+    up, far, down = me.to(x=x_up), me.to(x=x_far), me.to(x=x_down)
+    partners = [in_column((col + k) % 8) for k in range(1, 8)] + [z_up, z_down, up, far, down]
     barrier = pltpu.get_barrier_semaphore()
     for to in partners:
         pl.semaphore_signal(barrier, inc=1, device_id=to, device_id_type=MESH)
@@ -135,7 +134,7 @@
 
     pl.semaphore_wait(barrier, len(partners))
 
-    put_or_keep(straight, piece, raw.at[me.x, me.z], m_send, m_recv, mirrored[0])
+    put_or_keep(straight, piece, raw.at[me.x, me.z], m_send, m_recv, mirror)
 
     o, i = iota((192, 192), 0), iota((192, 192), 1)
     ordering = (((o % 48) // 12) * 48 + (o // 48) * 12 + o % 12 == i).astype(BF16)
@@ -150,15 +149,20 @@
         mine = raw.at[me.x, z_of(n)]
         put(mine, mine, d_send.at[n, 0], d_recv.at[n, 0], up)
         put(mine, mine, d_send.at[n, 1], d_recv.at[n, 1], down)
+        if direct(n):
+            put(mine, mine, l_send.at[n], l_recv.at[n], far)
+
+    def direct(n):
+        return (n if n < 8 else n - 7) >= DIRECT_FROM
 
     def pass_on(n):
         z = z_of(n)
         low, high = raw.at[x_down, z], raw.at[x_up, z]
         done(low, d_recv.at[n, 0])
-        if n < 8:
+        if n < 8 and not direct(n):
             put(low, low, l_send.at[n], l_recv.at[n], up)
         done(high, d_recv.at[n, 1])
-        if n >= 8:
+        if n >= 8 and not direct(n):
             put(high, high, l_send.at[n], l_recv.at[n], down)
 
     def settle(n):
@@ -183,8 +187,8 @@
         else:
             put_or_keep(straight, *args)
 
-    put_or_keep(straight, hist, events, hi_send.at[0], hi_recv.at[0], mirrored[0])
-    put_or_keep(straight, len_out, len_in, hi_send.at[1], hi_recv.at[1], mirrored[0])
+    put_or_keep(straight, hist, events, hi_send.at[0], hi_recv.at[0], mirror)
+    put_or_keep(straight, len_out, len_in, hi_send.at[1], hi_recv.at[1], mirror)
 
     def slots(shape, dim):
         slot = iota(shape, dim)
@@ -287,84 +291,81 @@
     source = ((o // 2) % 8) * 16 + (o % 2) * 8 + o // 16
     sorted_z[...] = mm((source == i).astype(BF16), got_y[...]).astype(BF16)
 
-    def pair_below(n, z):
-        return (zp + 8 - n + 2 * n * z) % 8
-
-    def send_z(n):
-        if n:
-            for first, p in ((0, (zp + n) % 8), (1, (zp + 8 - n) % 8)):
-                put(cut(sorted_z, p), rows.at[n, me.x, first, pl.ds(16 * z_lo, 16), :],
-                    z_send.at[n, first], z_recv.at[n, z_lo], me.to(z=p * 2 + first))
-        else:
-            p = (zp + 4) % 8
-            put(cut(sorted_z, p), rows.at[0, me.x, 1 - z_lo, pl.ds(16, 16), :],
-                z_send.at[0, 1], z_recv.at[0, 1], me.to(z=p * 2 + 1 - z_lo))
-            pltpu.make_async_copy(
-                cut(sorted_z, zp), rows.at[0, me.x, z_lo, pl.ds(0, 16), :], z_recv.at[0, 0]).start()
-
-    def share_own(n):
-        mine = rows.at[n, me.x, z_lo]
-        for h in range(2):
-            done(rows.at[n, me.x, z_lo, pl.ds(16 * h, 16), :], z_recv.at[n, h])
-        put(mine, mine, p_send.at[n], p_recv.at[n], mate)
-        put(mine, mine, g_send.at[n, 0, z_lo], g_recv.at[n, 0, z_lo], up)
-        put(mine, mine, g_send.at[n, 1, z_lo], g_recv.at[n, 1, z_lo], down)
-
-    def share_mate(n):
-        theirs = rows.at[n, me.x, 1 - z_lo]
-        done(theirs, p_recv.at[n])
-        put(theirs, theirs, g_send.at[n, 0, 1 - z_lo], g_recv.at[n, 0, 1 - z_lo], up)
-        put(theirs, theirs, g_send.at[n, 1, 1 - z_lo], g_recv.at[n, 1, 1 - z_lo], down)
-
-    def relay(n):
-        first, second = rows.at[n, x_down, 0], rows.at[n, x_up, 1]
-        done(first, g_recv.at[n, 0, 0])
-        put(first, first, r_send.at[n, 0], r_recv.at[n, 0], up)
-        done(second, g_recv.at[n, 1, 1])
-        put(second, second, r_send.at[n, 1], r_recv.at[n, 1], down)
-        done(rows.at[n, x_down, 1], g_recv.at[n, 0, 1])
-        done(rows.at[n, x_up, 0], g_recv.at[n, 1, 0])
-
-    def apply(n):
+    def send_z():
+        own = rows.at[0, me.x, z_lo]
+        pltpu.make_async_copy(cut(sorted_z, zp), own, z_recv.at[0]).start()
+        for n in Z_ORDER:
+            if n:
+                for first, p, s in ((0, (zp + n) % 8, 1 - z_lo), (1, (zp + 8 - n) % 8, z_lo)):
+                    put(cut(sorted_z, p), rows.at[2 * n + s, me.x, first],
+                        z_send.at[2 * n + first], z_recv.at[2 * n + s], me.to(z=p * 2 + first))
+            else:
+                p = (zp + 4) % 8
+                put(cut(sorted_z, p), rows.at[1, me.x, 1 - z_lo], z_send.at[1], z_recv.at[1], me.to(z=p * 2 + 1 - z_lo))
+
+    def share_own(q):
+        mine = rows.at[q, me.x, z_lo]
+        done(mine, z_recv.at[q])
+        put(mine, mine, p_send.at[q], p_recv.at[q], mate)
+        put(mine, mine, g_send.at[q, 0, z_lo], g_recv.at[q, 0, z_lo], up)
+        put(mine, mine, g_send.at[q, 1, z_lo], g_recv.at[q, 1, z_lo], down)
+
+    def share_mate(q):
+        theirs = rows.at[q, me.x, 1 - z_lo]
+        done(theirs, p_recv.at[q])
+        put(theirs, theirs, g_send.at[q, 0, 1 - z_lo], g_recv.at[q, 0, 1 - z_lo], up)
+        put(theirs, theirs, g_send.at[q, 1, 1 - z_lo], g_recv.at[q, 1, 1 - z_lo], down)
+
+    def relay(q):
+        first, second = rows.at[q, x_down, 0], rows.at[q, x_up, 1]
+        done(first, g_recv.at[q, 0, 0])
+        put(first, first, r_send.at[q, 0], r_recv.at[q, 0], up)
+        done(second, g_recv.at[q, 1, 1])
+        put(second, second, r_send.at[q, 1], r_recv.at[q, 1], down)
+        done(rows.at[q, x_down, 1], g_recv.at[q, 0, 1])
+        done(rows.at[q, x_up, 0], g_recv.at[q, 1, 0])
+
+    def apply(q):
         for b in range(2):
-            done(rows.at[n, x_far, b], r_recv.at[n, b])
-        if n == ORDER[0]:
+            done(rows.at[q, x_far, b], r_recv.at[q, b])
+        if q == ORDER[0]:
             for k, dst in enumerate((wg, wu, wd)):
                 done(dst, w_sem.at[k])
-        here = rows[n].reshape(256, D)
+        here = rows[q].reshape(128, D)
         gate, lift = mm(here, wg[...]), mm(here, wu[...])
         inner = (gate / (1.0 + jnp.exp(-gate)) * lift).astype(BF16)
-        res[n] = mm(inner, wd[...]).astype(BF16).reshape(4, 2, 32, D)
-        put(res.at[n, x_far, 0], halves.at[n, 0], h_send.at[n, 0], h_recv.at[n, 0], up)
-        put(res.at[n, x_far, 1], halves.at[n, 1], h_send.at[n, 1], h_recv.at[n, 1], down)
-
-    def add_halves(n):
+        res[q] = mm(inner, wd[...]).astype(BF16).reshape(4, 2, 16, D)
+        put(res.at[q, x_far, 0], halves.at[q, 0], h_send.at[q, 0], h_recv.at[q, 0], up)
+        put(res.at[q, x_far, 1], halves.at[q, 1], h_send.at[q, 1], h_recv.at[q, 1], down)
+
+    def add_halves(q):
         for b, x, to in ((0, x_up, up), (1, x_down, down)):
-            done(halves.at[n, b], h_recv.at[n, b])
-            res[n, x, b] = (res[n, x, b].astype(F32) + halves[n, b].astype(F32)).astype(BF16)
-            put(res.at[n, x], sums.at[n, b], s_send.at[n, b], s_recv.at[n, b], to)
-
-    def total(n, z):
-        return res[n, me.x, z].astype(F32) + sums[n, 0, z].astype(F32) + sums[n, 1, z].astype(F32)
-
-    def add_x(n):
+            done(halves.at[q, b], h_recv.at[q, b])
+            res[q, x, b] = (res[q, x, b].astype(F32) + halves[q, b].astype(F32)).astype(BF16)
+            put(res.at[q, x], sums.at[q, b], s_send.at[q, b], s_recv.at[q, b], to)
+
+    def total(q, z):
+        return res[q, me.x, z].astype(F32) + sums[q, 0, z].astype(F32) + sums[q, 1, z].astype(F32)
+
+    def add_x(q):
         for b in range(2):
-            done(sums.at[n, b], s_recv.at[n, b])
-        z_out[n] = total(n, 1 - z_lo).astype(BF16)
-        put(z_out.at[n], z_in.at[n], q_send.at[n], q_recv.at[n], mate)
-
-    def add_mate(n):
-        done(z_in.at[n], q_recv.at[n])
-        fin[n] = (total(n, z_lo) + z_in[n].astype(F32)).astype(BF16)
-        halves_of = [fin.at[n, pl.ds(16 * h, 16), :] for h in range(2)]
+            done(sums.at[q, b], s_recv.at[q, b])
+        z_out[q] = total(q, 1 - z_lo).astype(BF16)
+        put(z_out.at[q], z_in.at[q], q_send.at[q], q_recv.at[q], mate)
+
+    def add_mate(q):
+        done(z_in.at[q], q_recv.at[q])
+        fin[q] = (total(q, z_lo) + z_in[q].astype(F32)).astype(BF16)
+        n, s = q // 2, q % 2
         if n:
-            p = pair_below(n, z_lo)
-            for h in range(2):
-                put(halves_of[h], cut(back_z, zp), bz_send.at[n, h], bz_recv.at[n, z_lo], me.to(z=p * 2 + h))
+            p = (zp + 8 - n + 2 * n * z_lo) % 8
+            to = me.to(z=p * 2 + (1 - s) * (1 - z_lo) + s * z_lo)
+            put(fin.at[q], cut(back_z, zp), bz_send.at[q], bz_recv.at[2 * n + z_lo], to)
+        elif s:
+            p = (zp + 4) % 8
+            put(fin.at[1], cut(back_z, zp), bz_send.at[1], bz_recv.at[1], me.to(z=p * 2 + 1 - z_lo))
         else:
-            pltpu.make_async_copy(halves_of[0], cut(back_z, zp), bz_recv.at[0, 0]).start()
-            p = (zp + 4) % 8
-            put(halves_of[1], cut(back_z, zp), bz_send.at[0, 1], bz_recv.at[0, 1], me.to(z=p * 2 + 1 - z_lo))
+            pltpu.make_async_copy(fin.at[0], cut(back_z, zp), bz_recv.at[0]).start()
 
     def run(stages):
         for tick in range(CHUNKS + max(begin for _, begin in stages)):
@@ -372,16 +373,16 @@
                 if 0 <= tick - begin < CHUNKS:
                     stage(ORDER[tick - begin])
 
-    run(((send_z, 0), (share_own, LEAD), (share_mate, LEAD + FORWARD[0]), (relay, LEAD + FORWARD[1])))
-    run(((apply, 0), (add_halves, BACKWARD[0]), (add_x, BACKWARD[1]), (add_mate, BACKWARD[2])))
-
-    for n in range(CHUNKS):
+    send_z()
+    run(list(zip((share_own, share_mate, relay, apply, add_halves, add_x, add_mate), BEGIN)))
+
+    for n in range(4):
         if n:
-            done(cut(back_z, (zp + n) % 8), bz_recv.at[n, 0])
-            done(cut(back_z, (zp + 8 - n) % 8), bz_recv.at[n, 1])
+            done(cut(back_z, (zp + n) % 8), bz_recv.at[2 * n])
+            done(cut(back_z, (zp + 8 - n) % 8), bz_recv.at[2 * n + 1])
         else:
-            done(cut(back_z, zp), bz_recv.at[0, 0])
-            done(cut(back_z, (zp + 4) % 8), bz_recv.at[0, 1])
+            done(cut(back_z, zp), bz_recv.at[0])
+            done(cut(back_z, (zp + 4) % 8), bz_recv.at[1])
     source = (o % 8) * 16 + (o // 16) * 2 + (o // 8) % 2
     sorted_y[...] = mm((source == i).astype(BF16), back_z[...]).astype(BF16)
     pltpu.make_async_copy(cut(sorted_y, col), cut(back_y, col), by_recv.at[col]).start()
@@ -424,12 +425,12 @@
             vmem(8, 128, dtype=I32), vmem(8, 128, dtype=I32),
             vmem(48, OWN), vmem(4, 16, 48, OWN), vmem(4, D, OWN), vmem(4, ROWS, D), vmem(4, ROWS, D),
             vmem(D, OWN), vmem(D, OWN), vmem(OWN, D), vmem(128, D), vmem(128, D), vmem(128, D),
-            vmem(n, 4, 2, 32, D), vmem(n, 4, 2, 32, D), vmem(n, 2, 32, D), vmem(n, 2, 2, 32, D),
-            vmem(n, 32, D), vmem(n, 32, D), vmem(n, 32, D), vmem(128, D), vmem(128, D), vmem(128, D),
+            vmem(n, 4, 2, 16, D), vmem(n, 4, 2, 16, D), vmem(n, 2, 16, D), vmem(n, 2, 2, 16, D),
+            vmem(n, 16, D), vmem(n, 16, D), vmem(n, 16, D), vmem(128, D), vmem(128, D), vmem(128, D),
             ONE, dma(3), ONE, ONE, dma(4), dma(4), dma(2), dma(2),
             dma(8), dma(8), dma(8), dma(8), dma(16, 2), dma(16, 2), dma(16), dma(16), dma(16), ONE, dma(4), dma(4),
-            dma(8), dma(8), dma(n, 2), dma(n, 2), dma(n), dma(n), dma(n, 2, 2), dma(n, 2, 2), dma(n, 2), dma(n, 2),
-            dma(n, 2), dma(n, 2), dma(n, 2), dma(n, 2), dma(n), dma(n), dma(n, 2), dma(n, 2), dma(8), dma(8),
+            dma(8), dma(8), dma(n), dma(n), dma(n), dma(n), dma(n, 2, 2), dma(n, 2, 2), dma(n, 2), dma(n, 2),
+            dma(n, 2), dma(n, 2), dma(n, 2), dma(n, 2), dma(n), dma(n), dma(n), dma(n), dma(8), dma(8),
         ],
         compiler_params=pltpu.CompilerParams(
             collective_id=0, has_side_effects=True, vmem_limit_bytes=56 * 1024 * 1024

time: 163 us -> 154 us (0.945)
  Pallas kernels: 160 us -> 150 us
    pallas_call x1, Pallas kernels: 160 us -> 150 us  [shards(): pl.pallas_call(layer_kernel, out_shape=jax.ShapeDtypeStruct((ROWS, D), BF...]
where the time goes in v3:
time: 154 us; the launch traced here: 152 us
  Pallas kernels  150 us (97%)
  local copies, waits for them, and re-layouts  1.54 us (1%)
    pallas_call x1, Pallas kernels, shards(): pl.pallas_call(layer_kernel, out_shape=jax.ShapeDtypeStruct((ROWS, D), BF...  150 us

profile of v3, /device:TPU:1, one launch (start us, length us, event | category | flops | bytes accessed | tf_op | source)
XLA Modules:
  0.0 152.4 jit_solution(12463822200017875180)
XLA Ops:
  0.7 150.2 %layer.1 = bf16[32,1536]{1,0:T(8,128)(2,1)} custom-call(s32[1,32]{1,0:T(1,128)} %bitcast.19, s32[1]{0:T(128)S(6)} %copy.17.lens, s32[2,32]{1,0:T(2,128)} %bitcast.18, f32[1536]{0:T(1024)} %gain.1, f32[1536]{0:T(1024)} %moe_gain.1, bf16[12,384]{1,0:T(8,128)(2,1)} %w_key.1, bf16[12,384]{1,0:T(8,128)(2,1)} %w_value.1, bf16[12,384]{1,0:T(8,128)(2,1)} %w_query.1, ...), custom_call_target="tpu_custom_call" | custom-call | tf_op jit(solution)/shard_map/layer/pallas_call | solution.py:418
  150.9 1.5 %copy.18 = bf16[1,1,32,1536]{3,2,1,0:T(8,128)(2,1)} copy(bf16[1,1,32,1536]{3,2,1,0:T(8,128)(2,1)} %bitcast.15) | data formatting | bytes 196608

commit v4 on v3

--- a/solution.py
+++ b/solution.py
@@ -92,8 +92,9 @@
 
         sent.append((src, send, is_self))
 
-    def all_left():
-        for src, send, is_self in sent:
+    def all_left(but_last=0):
+        while len(sent) > but_last:
+            src, send, is_self = sent.pop(0)
             if is_self is None:
                 done(src, send)
             else:
@@ -126,11 +127,6 @@
     for m, ref in enumerate((w_key, w_value, w_query, w_out_t)):
         stacked += mm((o == i + 12 * m).astype(BF16), ref[...])
     piece[...] = stacked.astype(BF16)
-    len_out[...] = jnp.full((8, 128), lens[0], I32)
-    eye = (iota((ROWS, ROWS), 0) == iota((ROWS, ROWS), 1)).astype(BF16)
-    lookup = mm_nt(eye, (iota((256, ROWS), 0) == ids[...]).astype(BF16)).astype(BF16)
-    done(table, t_sem)
-    emb[...] = mm(lookup, table[...]).astype(BF16)
 
     pl.semaphore_wait(barrier, len(partners))
 
@@ -177,6 +173,12 @@
     put(own_piece, own_piece, f_send.at[0], f_recv.at[0], z_up)
     put(own_piece, own_piece, b_send.at[0], b_recv.at[0], z_down)
     share(0)
+
+    len_out[...] = jnp.full((8, 128), lens[0], I32)
+    eye = (iota((ROWS, ROWS), 0) == iota((ROWS, ROWS), 1)).astype(BF16)
+    lookup = mm_nt(eye, (iota((256, ROWS), 0) == ids[...]).astype(BF16)).astype(BF16)
+    done(table, t_sem)
+    emb[...] = mm(lookup, table[...]).astype(BF16)
 
     for k in range(4):
         y = (me.y + k) % 4
@@ -285,6 +287,7 @@
     powers = [jnp.exp(p - top) for p in picked]
     gates = [p / (powers[0] + powers[1]) for p in powers]
 
+    all_left(but_last=7)
     for k in range(8):
         done(cut(got_y, k), y_recv.at[k])
     o, i = iota((128, 128), 0), iota((128, 128), 1)
@@ -389,6 +392,7 @@
     for k in range(1, 8):
         d = (col + k) % 8
         put(cut(sorted_y, d), cut(back_y, col), by_send.at[k], by_recv.at[col], in_column(d))
+    all_left(but_last=7)
     for k in range(8):
         done(cut(back_y, k), by_recv.at[k])
 

time: 154 us -> 153 us (level); the launches traced: 152 us -> 153 us
  no operation moved by 1% of the time
where the time goes in v4:
time: 153 us
  Pallas kernels  151 us (99%)
  local copies, waits for them, and re-layouts  1.54 us (1%)
    pallas_call x1, Pallas kernels, shards(): pl.pallas_call(layer_kernel, out_shape=jax.ShapeDtypeStruct((ROWS, D), BF...  151 us

profile of v4, /device:TPU:1, one launch (start us, length us, event | category | flops | bytes accessed | tf_op | source)
XLA Modules:
  0.0 153.2 jit_solution(12681635076433615754)
XLA Ops:
  0.7 151.0 %layer.1 = bf16[32,1536]{1,0:T(8,128)(2,1)} custom-call(s32[1,32]{1,0:T(1,128)} %bitcast.19, s32[1]{0:T(128)S(6)} %copy.17.lens, s32[2,32]{1,0:T(2,128)} %bitcast.18, f32[1536]{0:T(1024)} %gain.1, f32[1536]{0:T(1024)} %moe_gain.1, bf16[12,384]{1,0:T(8,128)(2,1)} %w_key.1, bf16[12,384]{1,0:T(8,128)(2,1)} %w_value.1, bf16[12,384]{1,0:T(8,128)(2,1)} %w_query.1, ...), custom_call_target="tpu_custom_call" | custom-call | tf_op jit(solution)/shard_map/layer/pallas_call | solution.py:422
  151.6 1.5 %copy.18 = bf16[1,1,32,1536]{3,2,1,0:T(8,128)(2,1)} copy(bf16[1,1,32,1536]{3,2,1,0:T(8,128)(2,1)} %bitcast.15) | data formatting | bytes 196608

commit v5 on v4

--- a/solution.py
+++ b/solution.py
@@ -56,8 +56,8 @@
 Z_ORDER = (1, 2, 0, 3)
 CHUNKS = len(ORDER)
 BEGIN = (0, 1, 2, 3, 4, 5, 6)
-LAG = (2, 4)
-DIRECT_FROM = 6
+LAG = (2, 3)
+DIRECT_FROM = 5
 
 
 def layer_kernel(

time: 153 us -> 154 us (level)
  no operation moved by 1% of the time
where the time goes in v5:
time: 154 us
  Pallas kernels  152 us (99%)
  local copies, waits for them, and re-layouts  1.54 us (1%)
    pallas_call x1, Pallas kernels, shards(): pl.pallas_call(layer_kernel, out_shape=jax.ShapeDtypeStruct((ROWS, D), BF...  152 us

profile of v5, /device:TPU:1, one launch (start us, length us, event | category | flops | bytes accessed | tf_op | source)
XLA Modules:
  0.0 153.8 jit_solution(3601641312139220425)
XLA Ops:
  0.7 151.6 %layer.1 = bf16[32,1536]{1,0:T(8,128)(2,1)} custom-call(s32[1,32]{1,0:T(1,128)} %bitcast.19, s32[1]{0:T(128)S(6)} %copy.17.lens, s32[2,32]{1,0:T(2,128)} %bitcast.18, f32[1536]{0:T(1024)} %gain.1, f32[1536]{0:T(1024)} %moe_gain.1, bf16[12,384]{1,0:T(8,128)(2,1)} %w_key.1, bf16[12,384]{1,0:T(8,128)(2,1)} %w_value.1, bf16[12,384]{1,0:T(8,128)(2,1)} %w_query.1, ...), custom_call_target="tpu_custom_call" | custom-call | tf_op jit(solution)/shard_map/layer/pallas_call | solution.py:422
  152.2 1.5 %copy.18 = bf16[1,1,32,1536]{3,2,1,0:T(8,128)(2,1)} copy(bf16[1,1,32,1536]{3,2,1,0:T(8,128)(2,1)} %bitcast.15) | data formatting | bytes 196608
